TPU v7x, 512 devices: a whole 4x8x8 slice. The times are simulated.
512 devices in a mesh: ctx: 16 (over x, z_hi), dp: 8 (over y), tp: 4 (over z_lo, core).
Axes of the slice: x: 4, y: 8, z: 8 (z_hi: 4, z_lo: 2; z = z_hi * 2 + z_lo), core: 2. Of those that a mesh axis runs over, the one named last changes fastest.
Arguments:
- token_ids: int32 [4, 16], replicated, may hold values from 0 to 50279
- decode_prompt: int32 [16], replicated, may hold values from 0 to 15, as said below
- embedding: bfloat16 [50280, 4096], P('dp', ('ctx', 'tp')), may hold values from -6 to 6
- norm_gain: float32 [4096], replicated, may hold values from 0.1 to 1.9
- w_zx: bfloat16 [2, 128, 64, 4096], P(None, ('tp', 'ctx')), may hold values from -0.09375 to 0.09375
- w_bcdt: bfloat16 [4096, 384], P(None, ('ctx', 'tp')), may hold values from -0.09375 to 0.09375
- conv_x_weight: float32 [4, 128, 64], P(None, ('tp', 'ctx')), may hold values from -3 to 3
- conv_x_bias: float32 [128, 64], P(('tp', 'ctx')), may hold values from -3 to 3
- conv_bc_weight: float32 [4, 256], replicated, may hold values from -3 to 3
- conv_bc_bias: float32 [256], replicated, may hold values from -3 to 3
- dt_bias: float32 [128], P(('tp', 'ctx')), may hold values from -4 to -1
- a_log: float32 [128], P(('tp', 'ctx')), may hold values from 0 to 2.7
- d_skip: float32 [128], P(('tp', 'ctx')), may hold values from 0.5 to 1.5
- gate_norm_gain: float32 [128, 64], P(('tp', 'ctx')), may hold values from 0.1 to 1.9
- w_out: bfloat16 [128, 64, 4096], P(('tp', 'ctx')), may hold values from -0.0625 to 0.0625
- state_parts: bfloat16 [16, 16, 128, 64, 128], P('ctx', 'dp', 'tp'), may hold values from -6 to 6
- seg_rate: float32 [16, 16, 128], P('ctx', 'dp', 'tp'), may hold values from 0 to 2
- x_tail: bfloat16 [16, 3, 128, 64], P('dp', None, ('tp', 'ctx')), may hold values from -6 to 6
- bc_tail: bfloat16 [16, 3, 256], P('dp'), may hold values from -6 to 6
Outputs:
- mixer_out: bfloat16 [4, 16, 4096], P(None, 'dp', ('ctx', 'tp'))
- final_state: float32 [16, 128, 64, 128], P('dp', ('tp', 'ctx'))
Inputs may be any that keep to these rules, and one draw needn't show every extreme that they name: decode_prompt is a permutation of the prompts; slot s is decoded by dp group s // 2, and prompt q is held by dp group q // 2; the 2 prompts held by one dp group are decoded by 2 different dp groups.
All inputs are finite; a program needn't handle non-finite values.
Results may differ from a plain program's by a relative error of at most 0.02.
Values may be sent and summed in bfloat16 or wider, within the bound.
No kernel may reach another device: no remote copies, remote signals or barrier semaphores. Data moves between devices by JAX's collectives and lax.ppermute only.
A program may use at most 64 MiB of HBM per device.

v0:
```python
import jax
import jax.numpy as jnp
from jax import lax
from jax.sharding import PartitionSpec as P

HEADS = 128
HEAD_DIM = 64
epsilon = 1e-05


def from_everyone(shard, axis):
    count = lax.axis_size(axis)
    return lax.all_to_all(
        jnp.broadcast_to(shard[None], (count, *shard.shape)), axis, 0, 0, tiled=True
    )


def folded_in_pairs(pieces, combine):
    while len(jax.tree.leaves(pieces)[0]) > 1:
        pieces = jax.vmap(combine)(*(pieces[side::2] for side in (0, 1)))
    return pieces[0]


def prefix(shard, axis, combine, identity):
    count, here = (lax.axis_size(axis), lax.axis_index(axis))
    passed = jnp.arange(count) > here

    def kept(part, zero, own):
        part = jnp.where(
            passed.reshape(-1, *(1 for _ in own.shape)), part, jnp.asarray(zero, own.dtype)
        )
        return part[::-1]

    pieces = from_everyone(shard, axis)
    return folded_in_pairs(kept(pieces, identity, shard), combine)


def split_up(shard, dim, count):
    before, after = (shard.shape[:dim], shard.shape[dim + 1 :])
    return jnp.moveaxis(shard.reshape(*before, count, -1, *after), dim, 0)


def sum_at_owner(shard, axis, dim):
    count = lax.axis_size(axis)
    pieces = lax.all_to_all(split_up(shard, dim, count), axis, 0, 0, tiled=True)
    return jnp.sum(pieces.astype(jnp.float32), axis=0)


def rows_first(arrays, axis, dims):
    turned = [jnp.moveaxis(a, dim, 0) for a, dim in zip(arrays, dims)]
    widths = [t[0].size for t in turned]
    both = jnp.concatenate([t.reshape(-1, w) for t, w in zip(turned, widths)], axis=1)
    filled = lax.all_gather(both, axis, axis=0, tiled=True)
    pieces = jnp.split(filled, [sum(widths[:k]) for k in range(1, len(widths))], axis=1)
    return tuple(
        (
            jnp.moveaxis(b.reshape(-1, *t.shape[1:]), 0, dim)
            for b, t, dim in zip(pieces, turned, dims)
        )
    )


def laid_out(pieces, dim):
    dims = list(pieces.shape[1:])
    dims[dim] *= pieces.shape[0]
    return jnp.moveaxis(pieces, 0, dim).reshape(dims)


def collect(shard, axis, dim):
    pieces = from_everyone(shard, axis)
    return laid_out(pieces, dim)


def over_copies(shard, axis):
    everything = from_everyone(shard, axis)
    return jnp.sum(everything, axis=0)


def sum_at_owner_2(shard, axis, dim):
    pieces = split_up(shard, dim, lax.axis_size(axis))
    arrived = lax.all_to_all(pieces, axis, split_axis=0, concat_axis=0, tiled=True)
    return arrived.sum(axis=0)


def rms_scale(values, gain):
    return values * lax.rsqrt(jnp.mean(values * values, axis=-1, keepdims=True) + epsilon) * gain


def select_rows(picker, values):
    return jnp.tensordot(picker, values, axes=1, precision=lax.Precision.HIGHEST)


def add_rates(earlier, later_one):
    return earlier + later_one


def per_device(
    token_ids,
    decode_prompt,
    embedding,
    norm_gain,
    w_zx,
    w_bcdt,
    conv_x_weight,
    conv_x_bias,
    conv_bc_weight,
    conv_bc_bias,
    dt_bias,
    a_log,
    d_skip,
    gate_norm_gain,
    w_out,
    state_parts,
    seg_rate,
    x_tail,
    bc_tail,
):
    group = lax.axis_index("dp")
    local_count = state_parts.shape[1]
    slot_count = decode_prompt.shape[0]
    head_count = w_zx.shape[1]
    state_width = conv_bc_bias.shape[0] // 2
    after_rates = prefix(seg_rate, "ctx", add_rates, jnp.zeros_like(seg_rate))
    seg_weight = jnp.exp(-after_rates[0])
    scaled = seg_weight[:, :, None, None] * state_parts[0].astype(jnp.float32)
    combined = sum_at_owner(scaled.astype(jnp.bfloat16), "ctx", 1)
    tails_x = x_tail.astype(jnp.float32)
    tails_bc = bc_tail.astype(jnp.float32)
    own_slots = lax.dynamic_slice_in_dim(decode_prompt, group * local_count, local_count)
    prompt_ids = jnp.arange(slot_count, dtype=jnp.int32)
    every_state, every_x, every_bc = tuple(
        (
            part.astype(jnp.float32)
            for part in rows_first(
                (
                    combined.astype(jnp.bfloat16),
                    tails_x.astype(jnp.bfloat16),
                    tails_bc.astype(jnp.bfloat16),
                ),
                "dp",
                (0, 0, 0),
            )
        )
    )
    picker = (own_slots[:, None] == prompt_ids[None, :]).astype(jnp.float32)
    ssm_state = select_rows(picker, every_state)
    x_window = select_rows(picker, every_x)
    bc_window = select_rows(picker, every_bc)
    vocab_rows = embedding.shape[0]
    holder = (decode_prompt[:, None] == prompt_ids[None, :]).astype(jnp.int32)
    slot_tokens = jnp.sum(token_ids[:, None, :] * holder[None], axis=2)
    offset_tokens = slot_tokens - group * vocab_rows
    inside = (offset_tokens >= 0) & (offset_tokens < vocab_rows)
    looked = jnp.take(embedding, jnp.clip(offset_tokens, 0, vocab_rows - 1), axis=0)
    partial_rows = jnp.where(inside[..., None], looked.astype(jnp.float32), 0.0)
    own_rows = sum_at_owner(partial_rows.astype(jnp.bfloat16), "dp", 1)
    embedded = collect(own_rows.astype(jnp.bfloat16), ("ctx", "tp"), 2)
    steps_count = embedded.shape[0]
    flat_rows = embedded.reshape(-1, embedded.shape[2]).astype(jnp.float32)
    normed = rms_scale(flat_rows, norm_gain).astype(jnp.bfloat16)
    projected = jnp.einsum("rd,khed->krhe", normed, w_zx, preferred_element_type=jnp.float32)
    projected = projected.reshape(
        2, steps_count, local_count, projected.shape[2], projected.shape[3]
    )
    columns = collect(jnp.dot(normed, w_bcdt, preferred_element_type=jnp.float32), ("ctx", "tp"), 1)
    columns = columns.reshape(steps_count, local_count, -1)
    head_block = lax.axis_index("tp") * lax.axis_size("ctx") + lax.axis_index("ctx")
    head_start = 2 * state_width + head_block * head_count
    dt_raw = lax.dynamic_slice_in_dim(columns, head_start, head_count, 2)
    decay_rate = -jnp.exp(a_log)
    gated_steps = []
    for moment in range(steps_count):
        x_window = jnp.concatenate([x_window, projected[1, moment][:, None]], axis=1)
        bc_window = jnp.concatenate(
            [bc_window, columns[moment, :, None, : 2 * state_width]], axis=1
        )
        x_conv = jax.nn.silu(jnp.einsum("pkhe,khe->phe", x_window, conv_x_weight) + conv_x_bias)
        bc_conv = jax.nn.silu(jnp.einsum("pkn,kn->pn", bc_window, conv_bc_weight) + conv_bc_bias)
        step_size = jax.nn.softplus(dt_raw[moment] + dt_bias)
        retain = jnp.exp(step_size * decay_rate)
        ssm_state = (
            retain[:, :, None, None] * ssm_state
            + (step_size[:, :, None] * x_conv)[:, :, :, None] * bc_conv[:, None, None, :state_width]
        )
        output = (
            jnp.einsum("phen,pn->phe", ssm_state, bc_conv[:, state_width:])
            + d_skip[None, :, None] * x_conv
        )
        gated_steps.append(output * jax.nn.silu(projected[0, moment]))
        x_window = x_window[:, 1:]
        bc_window = bc_window[:, 1:]
    gated_all = jnp.stack(gated_steps)
    local_squares = jnp.sum(gated_all * gated_all, axis=(2, 3))
    total_squares = over_copies(local_squares, ("ctx", "tp"))
    inverse = lax.rsqrt(total_squares / (HEADS * HEAD_DIM) + epsilon)
    normed_out = (gated_all * inverse[:, :, None, None] * gate_norm_gain).astype(jnp.bfloat16)
    partial_out = jnp.einsum("tphe,hed->tpd", normed_out, w_out, preferred_element_type=jnp.float32)
    mixed = sum_at_owner_2(partial_out, ("ctx", "tp"), 2)
    return (mixed.astype(jnp.bfloat16), ssm_state)


def solution(mesh):
    return jax.shard_map(
        per_device,
        mesh=mesh,
        in_specs=(
            P(),
            P(),
            P("dp", ("ctx", "tp")),
            P(),
            P(None, ("tp", "ctx"), None, None),
            P(None, ("ctx", "tp")),
            P(None, ("tp", "ctx"), None),
            P(("tp", "ctx"), None),
            P(),
            P(),
            P(("tp", "ctx")),
            P(("tp", "ctx")),
            P(("tp", "ctx")),
            P(("tp", "ctx"), None),
            P(("tp", "ctx"), None, None),
            P("ctx", "dp", "tp", None, None),
            P("ctx", "dp", "tp"),
            P("dp", None, ("tp", "ctx"), None),
            P("dp", None, None),
        ),
        out_specs=(P(None, "dp", ("ctx", "tp")), P("dp", ("tp", "ctx"), None, None)),
        check_vma=False,
    )
```

profile of v0, /device:TPU:1, one launch (start us, length us, event | category | flops | bytes accessed | tf_op | source)
XLA Modules:
  0.0 178.2 jit_solution(10364687955391233364)
XLA Ops:
  0.6 1.4 broadcast_in_dim.52
  2.1 13.4 %all-to-all-start.3 = ((f32[16,1,2,32]{3,2,1,0:T(2,128)}), f32[16,1,2,32]{3,2,1,0:T(2,128)S(1)}, u32[]{:S(2)}, u32[]{:S(2)}) async-start(f32[16,1,2,32]{3,2,1,0:T(2,128)} %broadcast_in_dim.52), calls=%async_computation.3 | async-start | bytes 32768 | tf_op jit(solution)/shard_map/all_to_all | solution.py:13
  15.5 0.7 fusion.42
  16.2 0.8 multiply_reduce_fusion
  17.2 0.1 copy.221
  17.5 2.6 %copy.222 = bf16[6285,64]{1,0:T(8,128)(2,1)} copy(bf16[6285,64]{0,1:T(8,128)(2,1)} %param.21) | data formatting | bytes 1608960 | tf_op args[2]
  20.1 2.2 %gather_fusion = bf16[64,64]{1,0:T(8,128)(2,1)S(1)} fusion(bf16[6285,64]{1,0:T(8,128)(2,1)} %copy.222, s32[1024]{0:T(1024)S(1)} %pad_clamp_fusion), kind=kCustom, calls=%fused_computation | custom fusion | bytes 16640 | tf_op jit(solution)/shard_map/jit(_take)/gather | solution.py:154
  22.4 0.1 fusion.19
  22.5 0.7 reshape.439
  23.2 1.1 all-to-all-done.3
  24.3 6.8 %all-to-all-start = ((bf16[8,2,256]{2,1,0:T(2,128)(2,1)}), bf16[8,2,256]{2,1,0:T(2,128)(2,1)S(1)}, u32[]{:S(2)}, u32[]{:S(2)}) async-start(bf16[8,2,256]{2,1,0:T(2,128)(2,1)} %reshape.439), calls=%async_computation | async-start | bytes 16384 | tf_op jit(solution)/shard_map/all_to_all | solution.py:45
  31.3 6.4 %all-to-all-done = bf16[8,2,256]{2,1,0:T(2,128)(2,1)S(1)} async-done(((bf16[8,2,256]{2,1,0:T(2,128)(2,1)}), bf16[8,2,256]{2,1,0:T(2,128)(2,1)S(1)}, u32[]{:S(2)}, u32[]{:S(2)}) %all-to-all-start) | async-done | bytes 8224 | tf_op jit(solution)/shard_map/all_to_all | solution.py:45
  38.0 0.8 reshape.441
  38.7 11.3 %all-to-all-start.1 = ((bf16[64,2,256]{2,1,0:T(2,128)(2,1)}), bf16[64,2,256]{2,1,0:T(2,128)(2,1)S(1)}, u32[]{:S(2)}, u32[]{:S(2)}) async-start(bf16[64,2,256]{2,1,0:T(2,128)(2,1)} %reshape.441), calls=%async_computation.1 | async-start | bytes 131072 | tf_op jit(solution)/shard_map/all_to_all | solution.py:13
  50.2 9.7 %all-to-all-done.1 = bf16[64,2,256]{2,1,0:T(2,128)(2,1)S(1)} async-done(((bf16[64,2,256]{2,1,0:T(2,128)(2,1)}), bf16[64,2,256]{2,1,0:T(2,128)(2,1)S(1)}, u32[]{:S(2)}, u32[]{:S(2)}) %all-to-all-start.1) | async-done | bytes 65568 | tf_op jit(solution)/shard_map/all_to_all | solution.py:13
  59.9 0.1 reshape.442
  60.1 0.3 fusion.5
  60.4 0.1 reshape.396
  60.7 0.2 fusion.86
  60.9 0.8 broadcast_in_dim.49
  61.6 4.4 %all-to-all-start.2 = ((f32[64,8,6]{2,1,0:T(8,128)}), f32[64,8,6]{2,1,0:T(8,128)S(1)}, u32[]{:S(2)}, u32[]{:S(2)}) async-start(f32[64,8,6]{2,1,0:T(8,128)} %broadcast_in_dim.49), calls=%async_computation.2 | async-start | bytes 524288 | tf_op jit(solution)/shard_map/all_to_all | solution.py:13
  66.1 1.5 fusion.2
  67.6 1.1 copy.227
  68.7 9.4 %all-to-all-done.2 = f32[64,8,6]{2,1,0:T(8,128)S(1)} async-done(((f32[64,8,6]{2,1,0:T(8,128)}), f32[64,8,6]{2,1,0:T(8,128)S(1)}, u32[]{:S(2)}, u32[]{:S(2)}) %all-to-all-start.2) | async-done | bytes 12320 | tf_op jit(solution)/shard_map/all_to_all | solution.py:13
  78.1 4.8 %all-to-all-start.4 = ((bf16[16,2,2,64,128]{4,3,2,1,0:T(8,128)(2,1)}), bf16[16,2,2,64,128]{4,3,2,1,0:T(8,128)(2,1)S(1)}, u32[]{:S(2)}, u32[]{:S(2)}) async-start(bf16[16,2,2,64,128]{4,3,2,1,0:T(8,128)(2,1)} %copy.227), calls=%async_computation.4 | async-start | bytes 2097152 | tf_op jit(solution)/shard_map/all_to_all | solution.py:45
  82.9 0.6 reshape.389
  83.6 0.6 dynamic_slice.7
  84.2 0.5 exponential_negate_fusion
  84.7 1.6 fusion.12
  86.3 0.6 slice_bitcast_fusion.3
  86.9 0.8 copy.225
  87.7 1.1 reshape_reshape.4
  88.8 0.8 multiply_exponential_fusion.3
  90.0 0.7 copy.246
  90.7 0.7 copy.241
  91.4 0.6 copy.236
  92.0 0.7 copy.226
  92.7 0.6 slice_bitcast_fusion.5
  93.3 13.3 %all-to-all-done.4 = bf16[16,2,2,64,128]{4,3,2,1,0:T(8,128)(2,1)S(1)} async-done(((bf16[16,2,2,64,128]{4,3,2,1,0:T(8,128)(2,1)}), bf16[16,2,2,64,128]{4,3,2,1,0:T(8,128)(2,1)S(1)}, u32[]{:S(2)}, u32[]{:S(2)}) %all-to-all-start.4) | async-done | bytes 1048608 | tf_op jit(solution)/shard_map/all_to_all | solution.py:45
  106.6 0.2 reduce_sum.72
  106.9 20.3 %all-gather = bf16[8,2,17536]{2,1,0:T(2,128)(2,1)S(1)} all-gather(bf16[1,2,17536]{2,1,0:T(2,128)(2,1)S(1)} %maximum_bitcast_fusion), channel_id=1, replica_groups=mesh['ctx'=16,'dp'=8,'tp'=4] {'dp'}, dimensions={0}, use_global_device_ids=true | all-gather | bytes 631296 | tf_op jit(solution)/shard_map/all_gather | solution.py:53
  127.2 0.2 reshape.409
  127.6 0.2 fusion.17
  127.8 0.2 fusion.14
  128.1 0.6 broadcast_multiply_fusion.3
  128.8 0.1 copy.244
  129.3 0.7 fusion.35
  130.0 0.7 divide_multiply_fusion.10
  130.8 1.7 multiply_add_fusion
  132.5 0.1 fusion.10
  132.7 0.2 fusion.6
  132.8 0.2 fusion.8
  133.0 0.2 fusion.93
  133.5 26.3 %all_to_all.35 = f32[64,4,2]{1,2,0:T(2,128)S(1)} all-to-all(f32[64,4,2]{1,2,0:T(2,128)S(1)} %broadcast_in_dim.54), channel_id=1, replica_groups=mesh['ctx'=16,'dp'=8,'tp'=4] {'ctx','tp'}, dimensions={0} | all-to-all | bytes 4096 | tf_op jit(solution)/shard_map/all_to_all | solution.py:13
  160.0 0.8 multiply_convert_fusion.1
  160.8 0.3 convolution_bitcast_fusion
  161.1 0.2 reshape.395
  161.3 0.2 copy.372
  161.5 0.2 reshape.443
  161.7 14.2 %all_to_all.36 = f32[64,1,512]{2,1,0:T(1,128)S(1)} all-to-all(f32[64,1,512]{2,1,0:T(1,128)S(1)} %reshape.443), channel_id=1, replica_groups=mesh['ctx'=16,'dp'=8,'tp'=4] {'ctx','tp'}, dimensions={0} | all-to-all | bytes 262144 | tf_op jit(solution)/shard_map/all_to_all | solution.py:81
  175.9 0.5 broadcast.320
  176.4 0.9 reduce.20
  177.4 0.2 reshape.444
  177.7 0.6 copy.255
  (95 shorter events, 2.8 us)
Async XLA Ops:
  0.6 84.1 %copy-start = (bf16[2,2,64,4096]{3,2,1,0:T(8,128)(2,1)S(1)}, bf16[2,2,64,4096]{3,2,1,0:T(8,128)(2,1)}, u32[]{:S(2)}) copy-start(bf16[2,2,64,4096]{3,2,1,0:T(8,128)(2,1)} %param.23) | copy-start | bytes 6291460
  2.1 22.3 %all-to-all-start.3 = ((f32[16,1,2,32]{3,2,1,0:T(2,128)}), f32[16,1,2,32]{3,2,1,0:T(2,128)S(1)}, u32[]{:S(2)}, u32[]{:S(2)}) async-start(f32[16,1,2,32]{3,2,1,0:T(2,128)} %broadcast_in_dim.52), calls=%async_computation.3 | async-start | bytes 32768 | tf_op jit(solution)/shard_map/all_to_all | solution.py:13
  17.5 43.2 %copy-start.3 = (f32[4096]{0:T(1024)S(1)}, f32[4096]{0:T(1024)}, u32[]{:S(2)}) copy-start(f32[4096]{0:T(1024)} %param.22) | copy-start | bytes 49156
  17.5 43.2 %copy-start.4 = (bf16[4096,6]{0,1:T(8,128)(2,1)S(1)}, bf16[4096,6]{0,1:T(8,128)(2,1)}, u32[]{:S(2)}) copy-start(bf16[4096,6]{0,1:T(8,128)(2,1)} %param.24) | copy-start | bytes 147460
  24.3 13.4 %all-to-all-start = ((bf16[8,2,256]{2,1,0:T(2,128)(2,1)}), bf16[8,2,256]{2,1,0:T(2,128)(2,1)S(1)}, u32[]{:S(2)}, u32[]{:S(2)}) async-start(bf16[8,2,256]{2,1,0:T(2,128)(2,1)} %reshape.439), calls=%async_computation | async-start | bytes 16384 | tf_op jit(solution)/shard_map/all_to_all | solution.py:45
  38.7 21.1 %all-to-all-start.1 = ((bf16[64,2,256]{2,1,0:T(2,128)(2,1)}), bf16[64,2,256]{2,1,0:T(2,128)(2,1)S(1)}, u32[]{:S(2)}, u32[]{:S(2)}) async-start(bf16[64,2,256]{2,1,0:T(2,128)(2,1)} %reshape.441), calls=%async_computation.1 | async-start | bytes 131072 | tf_op jit(solution)/shard_map/all_to_all | solution.py:13
  60.7 8.1 %copy-start.11 = (f32[8]{0:T(128)}, f32[8]{0:T(128)S(1)}, u32[]{:S(2)}) copy-start(f32[8]{0:T(128)S(1)} %rsqrt.19) | copy-start | bytes 100
  61.6 16.5 %all-to-all-start.2 = ((f32[64,8,6]{2,1,0:T(8,128)}), f32[64,8,6]{2,1,0:T(8,128)S(1)}, u32[]{:S(2)}, u32[]{:S(2)}) async-start(f32[64,8,6]{2,1,0:T(8,128)} %broadcast_in_dim.49), calls=%async_computation.2 | async-start | bytes 524288 | tf_op jit(solution)/shard_map/all_to_all | solution.py:13
  67.6 15.4 %copy-start.13 = (bf16[2,3,2,64]{3,2,1,0:T(2,128)(2,1)S(1)}, bf16[2,3,2,64]{3,2,1,0:T(2,128)(2,1)}, u32[]{:S(2)}) copy-start(bf16[2,3,2,64]{3,2,1,0:T(2,128)(2,1)} %param.36) | copy-start | bytes 4612
  67.6 16.0 %copy-start.17 = (s32[16]{0:T(128)S(1)}, s32[16]{0:T(128)}, u32[]{:S(2)}) copy-start(s32[16]{0:T(128)} %param.20) | copy-start | bytes 196
  67.6 16.6 %copy-start.18 = (f32[2]{0:T(128)S(1)}, f32[2]{0:T(128)}, u32[]{:S(2)}) copy-start(f32[2]{0:T(128)} %param.30) | copy-start | bytes 28
  78.1 28.5 %all-to-all-start.4 = ((bf16[16,2,2,64,128]{4,3,2,1,0:T(8,128)(2,1)}), bf16[16,2,2,64,128]{4,3,2,1,0:T(8,128)(2,1)S(1)}, u32[]{:S(2)}, u32[]{:S(2)}) async-start(bf16[16,2,2,64,128]{4,3,2,1,0:T(8,128)(2,1)} %copy.227), calls=%async_computation.4 | async-start | bytes 2097152 | tf_op jit(solution)/shard_map/all_to_all | solution.py:45
  86.3 20.5 %copy-start.10 = (bf16[2,384]{1,0:T(2,128)(2,1)S(1)}, bf16[2,384]{1,0:T(2,128)(2,1)}, u32[]{:S(2)}) copy-start(bf16[2,384]{1,0:T(2,128)(2,1)} %reshape.389) | copy-start | bytes 4612
  86.3 20.5 %copy-start.14 = (bf16[2,3,256]{2,0,1:T(2,128)(2,1)S(1)}, bf16[2,3,256]{2,0,1:T(2,128)(2,1)}, u32[]{:S(2)}) copy-start(bf16[2,3,256]{2,0,1:T(2,128)(2,1)} %param.37) | copy-start | bytes 9220
  93.2 34.4 %copy-start.19 = (s32[2]{0:T(128)S(1)}, s32[2]{0:T(128)}, u32[]{:S(2)}) copy-start(s32[2]{0:T(128)} %dynamic_slice.7) | copy-start | bytes 28
  93.2 34.8 %copy-start.5 = (f32[2,1,2,64]{3,0,2,1:T(2,128)S(1)}, f32[2,1,2,64]{3,0,2,1:T(2,128)}, u32[]{:S(2)}) copy-start(f32[2,1,2,64]{3,0,2,1:T(2,128)} %get-tuple-element.51) | copy-start | bytes 3076
  93.2 34.8 %copy-start.12 = (f32[4,2,64]{2,1,0:T(2,128)S(1)}, f32[4,2,64]{2,1,0:T(2,128)}, u32[]{:S(2)}) copy-start(f32[4,2,64]{2,1,0:T(2,128)} %param.25) | copy-start | bytes 6148
  93.2 34.8 %copy-start.15 = (f32[2,64]{1,0:T(2,128)S(1)}, f32[2,64]{1,0:T(2,128)}, u32[]{:S(2)}) copy-start(f32[2,64]{1,0:T(2,128)} %param.26) | copy-start | bytes 1540
  130.8 2.4 %copy-start.6 = (f32[2,2,64]{2,0,1:T(2,128)S(1)}, f32[2,2,64]{2,0,1:T(2,128)}, u32[]{:S(2)}) copy-start(f32[2,2,64]{2,0,1:T(2,128)} %get-tuple-element.44) | copy-start | bytes 3076
  130.8 2.4 %copy-start.7 = (f32[2,2,64]{2,0,1:T(2,128)S(1)}, f32[2,2,64]{2,0,1:T(2,128)}, u32[]{:S(2)}) copy-start(f32[2,2,64]{2,0,1:T(2,128)} %get-tuple-element.76) | copy-start | bytes 3076
  130.8 2.4 %copy-start.8 = (f32[2,2,64]{2,0,1:T(2,128)S(1)}, f32[2,2,64]{2,0,1:T(2,128)}, u32[]{:S(2)}) copy-start(f32[2,2,64]{2,0,1:T(2,128)} %get-tuple-element.78) | copy-start | bytes 3076
  130.8 2.4 %copy-start.9 = (f32[2,2,64]{2,0,1:T(2,128)S(1)}, f32[2,2,64]{2,0,1:T(2,128)}, u32[]{:S(2)}) copy-start(f32[2,2,64]{2,0,1:T(2,128)} %get-tuple-element.80) | copy-start | bytes 3076
  130.8 2.4 %copy-start.16 = (f32[2]{0:T(128)S(1)}, f32[2]{0:T(128)}, u32[]{:S(2)}) copy-start(f32[2]{0:T(128)} %param.31) | copy-start | bytes 28
  130.8 30.0 %copy-start.1 = (bf16[2,64,4096]{2,1,0:T(8,128)(2,1)S(1)}, bf16[2,64,4096]{2,1,0:T(8,128)(2,1)}, u32[]{:S(2)}) copy-start(bf16[2,64,4096]{2,1,0:T(8,128)(2,1)} %param.33) | copy-start | bytes 3145732
  132.5 45.1 %copy-start.2 = (f32[2,2,64,128]{3,2,1,0:T(8,128)}, f32[2,2,64,128]{3,2,1,0:T(8,128)S(1)}, u32[]{:S(2)}) copy-start(f32[2,2,64,128]{3,2,1,0:T(8,128)S(1)} %copy.256) | copy-start | bytes 393220
where the time goes:
time: 179 us; the launch traced here: 178 us
  blocking collectives  60.8 us (34%)
  starting transfers between devices  40.8 us (23%)
  waiting for transfers between devices  40 us (22%)
  local copies, waits for them, and re-layouts  21.1 us (12%)
  other arithmetic  9.52 us (5%)
  matrix products  4.86 us (3%)
    all_to_all x3, starting transfers between devices, from_everyone(): lax.all_to_all(jnp.broadcast_to(shard[None], (count, *shard.shape)), axis...  29.2 us
    all_to_all x1, blocking collectives, from_everyone(): lax.all_to_all(jnp.broadcast_to(shard[None], (count, *shard.shape)), axis...  26.3 us
    all_gather x1, blocking collectives, rows_first(): filled = lax.all_gather(both, axis, axis=0, tiled=True)  20.3 us
    all_to_all x3, waiting for transfers between devices, from_everyone(): lax.all_to_all(jnp.broadcast_to(shard[None], (count, *shard.shape)), axis...  20.2 us
    all_to_all x2, waiting for transfers between devices, sum_at_owner(): pieces = lax.all_to_all(split_up(shard, dim, count), axis, 0, 0, tiled=True)  19.8 us
    all_to_all x1, blocking collectives, sum_at_owner_2(): lax.all_to_all(pieces, axis, split_axis=0, concat_axis=0, tiled=True)  14.2 us
    all_to_all x2, starting transfers between devices, sum_at_owner(): pieces = lax.all_to_all(split_up(shard, dim, count), axis, 0, 0, tiled=True)  11.6 us
    unnamed x53, local copies, waits for them, and re-layouts  5.79 us
  transfers between devices with their start and end apart: 5, of which 5 were waited for; matrix products, arithmetic and copies ran while one was open for 12% of the time, Pallas kernels for 0%

commit v1 on v0

--- a/solution.py
+++ b/solution.py
@@ -50,7 +50,8 @@
     turned = [jnp.moveaxis(a, dim, 0) for a, dim in zip(arrays, dims)]
     widths = [t[0].size for t in turned]
     both = jnp.concatenate([t.reshape(-1, w) for t, w in zip(turned, widths)], axis=1)
-    filled = lax.all_gather(both, axis, axis=0, tiled=True)
+    repeated = jnp.stack([both] * lax.axis_size(axis))
+    filled = jnp.concatenate(lax.all_to_all(repeated, axis, 0, 0), axis=0)
     pieces = jnp.split(filled, [sum(widths[:k]) for k in range(1, len(widths))], axis=1)
     return tuple(
         (

time: 179 us -> 177 us (0.989)
  blocking collectives: 60.8 us -> 29.9 us
  waiting for transfers between devices: 40 us -> 65.8 us
  starting transfers between devices: 40.8 us -> 43.9 us
  other arithmetic: 9.52 us -> 7.71 us
    all_gather x1 -> x0, blocking collectives: 20.3 us -> none  [rows_first(): filled = lax.all_gather(both, axis, axis=0, tiled=True)]
    all_to_all x2, waiting for transfers between devices: 19.8 us -> 33.1 us  [sum_at_owner(): pieces = lax.all_to_all(split_up(shard, dim, count), axis, 0, 0, tiled=True)]
    all_to_all x0 -> x1, waiting for transfers between devices: none -> 13 us  [rows_first(): filled = jnp.concatenate(lax.all_to_all(repeated, axis, 0, 0), axis=0)]
    all_to_all x1, blocking collectives: 26.3 us -> 15.6 us  [from_everyone(): lax.all_to_all(jnp.broadcast_to(shard[None], (count, *shard.shape)), axis...]
    all_to_all x0 -> x1, starting transfers between devices: none -> 3.67 us  [rows_first(): filled = jnp.concatenate(lax.all_to_all(repeated, axis, 0, 0), axis=0)]
    unnamed x53 -> x50, local copies, waits for them, and re-layouts: 5.79 us -> 6.38 us
  transfers between devices with their start and end apart: 5 -> 6, of which waited for: 5 -> 6; matrix products, arithmetic and copies ran while one was open for 12% -> 11% of each run, Pallas kernels for 0% -> 0%
where the time goes in v1:
time: 177 us; the launch traced here: 176 us
  waiting for transfers between devices  65.8 us (37%)
  starting transfers between devices  43.9 us (25%)
  blocking collectives  29.9 us (17%)
  local copies, waits for them, and re-layouts  21.2 us (12%)
  other arithmetic  7.71 us (4%)
  matrix products  6.19 us (3%)
    all_to_all x2, waiting for transfers between devices, sum_at_owner(): pieces = lax.all_to_all(split_up(shard, dim, count), axis, 0, 0, tiled=True)  33.1 us
    all_to_all x3, starting transfers between devices, from_everyone(): lax.all_to_all(jnp.broadcast_to(shard[None], (count, *shard.shape)), axis...  29.8 us
    all_to_all x3, waiting for transfers between devices, from_everyone(): lax.all_to_all(jnp.broadcast_to(shard[None], (count, *shard.shape)), axis...  19.8 us
    all_to_all x1, blocking collectives, from_everyone(): lax.all_to_all(jnp.broadcast_to(shard[None], (count, *shard.shape)), axis...  15.6 us
    all_to_all x1, blocking collectives, sum_at_owner_2(): lax.all_to_all(pieces, axis, split_axis=0, concat_axis=0, tiled=True)  14.2 us
    all_to_all x1, waiting for transfers between devices, rows_first(): filled = jnp.concatenate(lax.all_to_all(repeated, axis, 0, 0), axis=0)  13 us
    all_to_all x2, starting transfers between devices, sum_at_owner(): pieces = lax.all_to_all(split_up(shard, dim, count), axis, 0, 0, tiled=True)  10.5 us
    unnamed x50, local copies, waits for them, and re-layouts  6.38 us
  transfers between devices with their start and end apart: 6, of which 6 were waited for; matrix products, arithmetic and copies ran while one was open for 11% of the time, Pallas kernels for 0%

profile of v1, /device:TPU:1, one launch (start us, length us, event | category | flops | bytes accessed | tf_op | source)
XLA Modules:
  0.0 176.0 jit_solution(3919949579159300642)
XLA Ops:
  0.7 1.4 broadcast_in_dim.52
  2.1 13.4 %all-to-all-start.3 = ((f32[16,1,2,32]{3,2,1,0:T(2,128)}), f32[16,1,2,32]{3,2,1,0:T(2,128)S(1)}, u32[]{:S(2)}, u32[]{:S(2)}) async-start(f32[16,1,2,32]{3,2,1,0:T(2,128)} %broadcast_in_dim.52), calls=%async_computation.3 | async-start | bytes 32768 | tf_op jit(solution)/shard_map/all_to_all | solution.py:13
  15.5 0.7 fusion.42
  16.3 0.8 multiply_reduce_fusion
  17.2 0.1 copy.217
  17.5 2.5 %copy.218 = bf16[6285,64]{1,0:T(8,128)(2,1)} copy(bf16[6285,64]{0,1:T(8,128)(2,1)} %param.21) | data formatting | bytes 1608960 | tf_op args[2]
  20.1 2.2 %gather_fusion = bf16[64,64]{1,0:T(8,128)(2,1)S(1)} fusion(bf16[6285,64]{1,0:T(8,128)(2,1)} %copy.218, s32[1024]{0:T(1024)S(1)} %pad_clamp_fusion), kind=kCustom, calls=%fused_computation | custom fusion | bytes 16640 | tf_op jit(solution)/shard_map/jit(_take)/gather | solution.py:155
  22.3 0.1 fusion.19
  22.5 0.7 reshape.443
  23.2 1.2 all-to-all-done.3
  24.4 6.8 %all-to-all-start = ((bf16[8,2,256]{2,1,0:T(2,128)(2,1)}), bf16[8,2,256]{2,1,0:T(2,128)(2,1)S(1)}, u32[]{:S(2)}, u32[]{:S(2)}) async-start(bf16[8,2,256]{2,1,0:T(2,128)(2,1)} %reshape.443), calls=%async_computation | async-start | bytes 16384 | tf_op jit(solution)/shard_map/all_to_all | solution.py:45
  31.4 6.3 %all-to-all-done = bf16[8,2,256]{2,1,0:T(2,128)(2,1)S(1)} async-done(((bf16[8,2,256]{2,1,0:T(2,128)(2,1)}), bf16[8,2,256]{2,1,0:T(2,128)(2,1)S(1)}, u32[]{:S(2)}, u32[]{:S(2)}) %all-to-all-start) | async-done | bytes 8224 | tf_op jit(solution)/shard_map/all_to_all | solution.py:45
  38.0 0.8 reshape.445
  38.8 11.3 %all-to-all-start.1 = ((bf16[64,2,256]{2,1,0:T(2,128)(2,1)}), bf16[64,2,256]{2,1,0:T(2,128)(2,1)S(1)}, u32[]{:S(2)}, u32[]{:S(2)}) async-start(bf16[64,2,256]{2,1,0:T(2,128)(2,1)} %reshape.445), calls=%async_computation.1 | async-start | bytes 131072 | tf_op jit(solution)/shard_map/all_to_all | solution.py:13
  50.0 0.3 fusion.2
  50.3 1.1 copy.223
  51.5 8.4 %all-to-all-done.1 = bf16[64,2,256]{2,1,0:T(2,128)(2,1)S(1)} async-done(((bf16[64,2,256]{2,1,0:T(2,128)(2,1)}), bf16[64,2,256]{2,1,0:T(2,128)(2,1)S(1)}, u32[]{:S(2)}, u32[]{:S(2)}) %all-to-all-start.1) | async-done | bytes 65568 | tf_op jit(solution)/shard_map/all_to_all | solution.py:13
  59.8 3.7 %all-to-all-start.4 = ((bf16[16,2,2,64,128]{4,3,2,1,0:T(8,128)(2,1)}), bf16[16,2,2,64,128]{4,3,2,1,0:T(8,128)(2,1)S(1)}, u32[]{:S(2)}, u32[]{:S(2)}) async-start(bf16[16,2,2,64,128]{4,3,2,1,0:T(8,128)(2,1)} %copy.223), calls=%async_computation.4 | async-start | bytes 2097152 | tf_op jit(solution)/shard_map/all_to_all | solution.py:45
  63.6 0.1 reshape.446
  63.8 0.8 copy.220
  64.6 1.1 reshape.402
  65.7 0.3 fusion.5
  66.1 0.2 fusion.86
  66.3 26.7 %all-to-all-done.4 = bf16[16,2,2,64,128]{4,3,2,1,0:T(8,128)(2,1)S(1)} async-done(((bf16[16,2,2,64,128]{4,3,2,1,0:T(8,128)(2,1)}), bf16[16,2,2,64,128]{4,3,2,1,0:T(8,128)(2,1)S(1)}, u32[]{:S(2)}, u32[]{:S(2)}) %all-to-all-start.4) | async-done | bytes 1048608 | tf_op jit(solution)/shard_map/all_to_all | solution.py:45
  93.0 0.7 broadcast_in_dim.49
  93.7 5.1 %all-to-all-start.2 = ((f32[64,8,6]{2,1,0:T(8,128)}), f32[64,8,6]{2,1,0:T(8,128)S(1)}, u32[]{:S(2)}, u32[]{:S(2)}) async-start(f32[64,8,6]{2,1,0:T(8,128)} %broadcast_in_dim.49), calls=%async_computation.2 | async-start | bytes 524288 | tf_op jit(solution)/shard_map/all_to_all | solution.py:13
  98.8 0.8 reduce_sum.72
  99.7 0.9 copy.366
  100.7 10.2 %all-to-all-done.2 = f32[64,8,6]{2,1,0:T(8,128)S(1)} async-done(((f32[64,8,6]{2,1,0:T(8,128)}), f32[64,8,6]{2,1,0:T(8,128)S(1)}, u32[]{:S(2)}, u32[]{:S(2)}) %all-to-all-start.2) | async-done | bytes 12320 | tf_op jit(solution)/shard_map/all_to_all | solution.py:13
  110.9 1.1 stack.12
  112.0 3.7 %all-to-all-start.5 = ((bf16[8,2,17536]{2,1,0:T(2,128)(2,1)}), bf16[8,2,17536]{2,1,0:T(2,128)(2,1)S(1)}, u32[]{:S(2)}, u32[]{:S(2)}) async-start(bf16[8,2,17536]{2,1,0:T(2,128)(2,1)} %stack.12), calls=%async_computation.5 | async-start | bytes 1122304 | tf_op jit(solution)/shard_map/all_to_all | solution.py:54
  115.7 0.7 dynamic_slice.7
  116.3 1.6 fusion.12
  118.1 0.2 reshape_reshape.4
  118.3 0.1 multiply_exponential_fusion.3
  118.8 0.6 copy.241
  119.4 0.6 copy.236
  120.0 0.7 copy.231
  120.7 0.7 copy.222
  121.4 13.0 %all-to-all-done.5 = bf16[8,2,17536]{2,1,0:T(2,128)(2,1)S(1)} async-done(((bf16[8,2,17536]{2,1,0:T(2,128)(2,1)}), bf16[8,2,17536]{2,1,0:T(2,128)(2,1)S(1)}, u32[]{:S(2)}, u32[]{:S(2)}) %all-to-all-start.5) | async-done | bytes 561184 | tf_op jit(solution)/shard_map/all_to_all | solution.py:54
  134.3 0.2 reshape.396
  134.7 0.8 fusion.17
  135.6 0.8 fusion.14
  136.5 1.3 broadcast_multiply_fusion.3
  137.9 0.1 copy.239
  138.0 0.1 copy.234
  138.1 0.1 copy.228
  138.4 0.7 divide_multiply_fusion.10
  139.2 1.7 multiply_add_fusion
  141.0 0.1 fusion.10
  141.1 0.2 fusion.6
  141.3 0.2 fusion.8
  141.4 0.2 fusion.93
  142.0 15.6 %all_to_all.40 = f32[64,4,2]{1,2,0:T(2,128)S(1)} all-to-all(f32[64,4,2]{1,2,0:T(2,128)S(1)} %broadcast_in_dim.54), channel_id=1, replica_groups=mesh['ctx'=16,'dp'=8,'tp'=4] {'ctx','tp'}, dimensions={0} | all-to-all | bytes 4096 | tf_op jit(solution)/shard_map/all_to_all | solution.py:13
  157.8 0.8 multiply_convert_fusion.1
  158.6 0.3 convolution_bitcast_fusion
  158.9 0.2 reshape.401
  159.1 0.2 copy.367
  159.2 0.2 reshape.447
  159.5 14.2 %all_to_all.41 = f32[64,1,512]{2,1,0:T(1,128)S(1)} all-to-all(f32[64,1,512]{2,1,0:T(1,128)S(1)} %reshape.447), channel_id=1, replica_groups=mesh['ctx'=16,'dp'=8,'tp'=4] {'ctx','tp'}, dimensions={0} | all-to-all | bytes 262144 | tf_op jit(solution)/shard_map/all_to_all | solution.py:82
  173.7 0.5 broadcast.322
  174.2 0.9 reduce.20
  175.2 0.2 reshape.448
  175.4 0.6 copy.250
  (95 shorter events, 2.6 us)
Async XLA Ops:
  0.6 115.7 %copy-start = (bf16[2,2,64,4096]{3,2,1,0:T(8,128)(2,1)S(1)}, bf16[2,2,64,4096]{3,2,1,0:T(8,128)(2,1)}, u32[]{:S(2)}) copy-start(bf16[2,2,64,4096]{3,2,1,0:T(8,128)(2,1)} %param.23) | copy-start | bytes 6291460
  0.6 49.4 %copy-start.2 = (bf16[1,2,32,64,128]{4,3,2,1,0:T(8,128)(2,1)S(1)}, bf16[1,2,32,64,128]{4,3,2,1,0:T(8,128)(2,1)}, u32[]{:S(2)}) copy-start(bf16[1,2,32,64,128]{4,3,2,1,0:T(8,128)(2,1)} %param.34) | copy-start | bytes 3145732
  2.1 22.3 %all-to-all-start.3 = ((f32[16,1,2,32]{3,2,1,0:T(2,128)}), f32[16,1,2,32]{3,2,1,0:T(2,128)S(1)}, u32[]{:S(2)}, u32[]{:S(2)}) async-start(f32[16,1,2,32]{3,2,1,0:T(2,128)} %broadcast_in_dim.52), calls=%async_computation.3 | async-start | bytes 32768 | tf_op jit(solution)/shard_map/all_to_all | solution.py:13
  24.4 13.4 %all-to-all-start = ((bf16[8,2,256]{2,1,0:T(2,128)(2,1)}), bf16[8,2,256]{2,1,0:T(2,128)(2,1)S(1)}, u32[]{:S(2)}, u32[]{:S(2)}) async-start(bf16[8,2,256]{2,1,0:T(2,128)(2,1)} %reshape.443), calls=%async_computation | async-start | bytes 16384 | tf_op jit(solution)/shard_map/all_to_all | solution.py:45
  38.8 21.1 %all-to-all-start.1 = ((bf16[64,2,256]{2,1,0:T(2,128)(2,1)}), bf16[64,2,256]{2,1,0:T(2,128)(2,1)S(1)}, u32[]{:S(2)}, u32[]{:S(2)}) async-start(bf16[64,2,256]{2,1,0:T(2,128)(2,1)} %reshape.445), calls=%async_computation.1 | async-start | bytes 131072 | tf_op jit(solution)/shard_map/all_to_all | solution.py:13
  50.3 13.2 %copy-start.13 = (bf16[2,3,2,64]{3,2,1,0:T(2,128)(2,1)S(1)}, bf16[2,3,2,64]{3,2,1,0:T(2,128)(2,1)}, u32[]{:S(2)}) copy-start(bf16[2,3,2,64]{3,2,1,0:T(2,128)(2,1)} %param.36) | copy-start | bytes 4612
  51.4 14.6 %copy-start.4 = (f32[4096]{0:T(1024)S(1)}, f32[4096]{0:T(1024)}, u32[]{:S(2)}) copy-start(f32[4096]{0:T(1024)} %param.22) | copy-start | bytes 49156
  51.5 14.6 %copy-start.5 = (bf16[4096,6]{0,1:T(8,128)(2,1)S(1)}, bf16[4096,6]{0,1:T(8,128)(2,1)}, u32[]{:S(2)}) copy-start(bf16[4096,6]{0,1:T(8,128)(2,1)} %param.24) | copy-start | bytes 147460
  59.8 33.2 %all-to-all-start.4 = ((bf16[16,2,2,64,128]{4,3,2,1,0:T(8,128)(2,1)}), bf16[16,2,2,64,128]{4,3,2,1,0:T(8,128)(2,1)S(1)}, u32[]{:S(2)}, u32[]{:S(2)}) async-start(bf16[16,2,2,64,128]{4,3,2,1,0:T(8,128)(2,1)} %copy.223), calls=%async_computation.4 | async-start | bytes 2097152 | tf_op jit(solution)/shard_map/all_to_all | solution.py:45
  63.5 37.1 %copy-start.14 = (bf16[2,3,256]{2,0,1:T(2,128)(2,1)S(1)}, bf16[2,3,256]{2,0,1:T(2,128)(2,1)}, u32[]{:S(2)}) copy-start(bf16[2,3,256]{2,0,1:T(2,128)(2,1)} %param.37) | copy-start | bytes 9220
  66.0 49.7 %copy-start.18 = (f32[2]{0:T(128)S(1)}, f32[2]{0:T(128)}, u32[]{:S(2)}) copy-start(f32[2]{0:T(128)} %param.30) | copy-start | bytes 28
  66.1 27.7 %copy-start.10 = (f32[8]{0:T(128)}, f32[8]{0:T(128)S(1)}, u32[]{:S(2)}) copy-start(f32[8]{0:T(128)S(1)} %rsqrt.19) | copy-start | bytes 100
  66.1 49.6 %copy-start.16 = (s32[16]{0:T(128)S(1)}, s32[16]{0:T(128)}, u32[]{:S(2)}) copy-start(s32[16]{0:T(128)} %param.20) | copy-start | bytes 196
  93.7 17.1 %all-to-all-start.2 = ((f32[64,8,6]{2,1,0:T(8,128)}), f32[64,8,6]{2,1,0:T(8,128)S(1)}, u32[]{:S(2)}, u32[]{:S(2)}) async-start(f32[64,8,6]{2,1,0:T(8,128)} %broadcast_in_dim.49), calls=%async_computation.2 | async-start | bytes 524288 | tf_op jit(solution)/shard_map/all_to_all | solution.py:13
  112.0 6.3 %copy-start.17 = (f32[2]{0:T(128)S(1)}, f32[2]{0:T(128)}, u32[]{:S(2)}) copy-start(f32[2]{0:T(128)} %param.29) | copy-start | bytes 28
  112.0 22.4 %all-to-all-start.5 = ((bf16[8,2,17536]{2,1,0:T(2,128)(2,1)}), bf16[8,2,17536]{2,1,0:T(2,128)(2,1)S(1)}, u32[]{:S(2)}, u32[]{:S(2)}) async-start(bf16[8,2,17536]{2,1,0:T(2,128)(2,1)} %stack.12), calls=%async_computation.5 | async-start | bytes 1122304 | tf_op jit(solution)/shard_map/all_to_all | solution.py:54
  118.0 18.5 %copy-start.11 = (f32[4,2,64]{2,1,0:T(2,128)S(1)}, f32[4,2,64]{2,1,0:T(2,128)}, u32[]{:S(2)}) copy-start(f32[4,2,64]{2,1,0:T(2,128)} %param.25) | copy-start | bytes 6148
  118.1 20.3 %copy-start.12 = (f32[4,256]{1,0:T(4,128)S(1)}, f32[4,256]{1,0:T(4,128)}, u32[]{:S(2)}) copy-start(f32[4,256]{1,0:T(4,128)} %param.27) | copy-start | bytes 12292
  139.2 2.4 %copy-start.6 = (f32[2,2,64]{2,0,1:T(2,128)S(1)}, f32[2,2,64]{2,0,1:T(2,128)}, u32[]{:S(2)}) copy-start(f32[2,2,64]{2,0,1:T(2,128)} %get-tuple-element.44) | copy-start | bytes 3076
  139.2 2.4 %copy-start.7 = (f32[2,2,64]{2,0,1:T(2,128)S(1)}, f32[2,2,64]{2,0,1:T(2,128)}, u32[]{:S(2)}) copy-start(f32[2,2,64]{2,0,1:T(2,128)} %get-tuple-element.76) | copy-start | bytes 3076
  139.2 2.4 %copy-start.8 = (f32[2,2,64]{2,0,1:T(2,128)S(1)}, f32[2,2,64]{2,0,1:T(2,128)}, u32[]{:S(2)}) copy-start(f32[2,2,64]{2,0,1:T(2,128)} %get-tuple-element.78) | copy-start | bytes 3076
  139.2 2.4 %copy-start.9 = (f32[2,2,64]{2,0,1:T(2,128)S(1)}, f32[2,2,64]{2,0,1:T(2,128)}, u32[]{:S(2)}) copy-start(f32[2,2,64]{2,0,1:T(2,128)} %get-tuple-element.80) | copy-start | bytes 3076
  139.2 2.4 %copy-start.15 = (f32[2]{0:T(128)S(1)}, f32[2]{0:T(128)}, u32[]{:S(2)}) copy-start(f32[2]{0:T(128)} %param.31) | copy-start | bytes 28
  139.2 19.3 %copy-start.1 = (bf16[2,64,4096]{2,1,0:T(8,128)(2,1)S(1)}, bf16[2,64,4096]{2,1,0:T(8,128)(2,1)}, u32[]{:S(2)}) copy-start(bf16[2,64,4096]{2,1,0:T(8,128)(2,1)} %param.33) | copy-start | bytes 3145732
  141.0 34.5 %copy-start.3 = (f32[2,2,64,128]{3,2,1,0:T(8,128)}, f32[2,2,64,128]{3,2,1,0:T(8,128)S(1)}, u32[]{:S(2)}) copy-start(f32[2,2,64,128]{3,2,1,0:T(8,128)S(1)} %copy.251) | copy-start | bytes 393220
